TPU v7x, 32 devices: a whole 2x2x4 slice. The times are simulated.
32 devices in a mesh: row: 4 (over x, core), col: 8 (over z, y).
Axes of the slice: x: 2, y: 2, z: 4, core: 2. Of those that a mesh axis runs over, the one named last changes fastest.
Arguments:
- first_alignment_matrix: float32 [16, 128, 32], P('row', 'col'), may hold values from -6 to 6
- second_alignment_matrix: float32 [16, 128, 32], P('row', 'col'), may hold values from -6 to 6
- couple_delta_sensitivity: float32 [128, 128, 128], P('row', 'col'), may hold values from -6 to 6
- mapping_matrix: float32 [1024, 128], replicated, may hold values from -0.1875 to 0.1875
Outputs:
- grad_left: float32 [16, 128, 32], P('row', 'col')
- grad_right: float32 [16, 128, 32], P('row', 'col')
All inputs are finite; a program needn't handle non-finite values.
Results may differ from a plain program's by a relative error of at most 0.0003.
Values sent between devices are 32-bit elements; how exact they have to be, the bound alone decides.
A program may use at most 64 MiB of HBM per device.

v0:
```python
import jax
import jax.numpy as jnp
from jax import lax
from jax.sharding import PartitionSpec as P


def on_device(
    first_alignment_matrix, second_alignment_matrix, couple_delta_sensitivity, mapping_matrix
):
    exact_arithmetic = lax.Precision.HIGHEST
    sequences_on_device = first_alignment_matrix.shape[0]
    row_count = lax.axis_size("row")
    summed_extent = sequences_on_device * row_count
    first_feature_number = first_alignment_matrix.shape[2]
    second_feature_number = second_alignment_matrix.shape[2]
    pair_chans = couple_delta_sensitivity.shape[2]
    tile_i = couple_delta_sensitivity.shape[0]
    tile_j = couple_delta_sensitivity.shape[1]
    second_collected = lax.all_gather(second_alignment_matrix, "row", axis=0, tiled=True)
    second_flat = second_collected.reshape(summed_extent, tile_j * second_feature_number)
    expanded_outer_term = lax.all_gather(first_alignment_matrix, "col", axis=1, tiled=True)
    left_all = lax.all_to_all(expanded_outer_term, "row", split_axis=1, concat_axis=0, tiled=True)
    weight3 = mapping_matrix.reshape(first_feature_number, second_feature_number, pair_chans)
    block_rows = tile_i // 4
    grad_blocks = couple_delta_sensitivity.reshape(4, block_rows, tile_j, pair_chans)
    left_blocks = jnp.transpose(
        left_all.reshape(summed_extent, 4, block_rows, first_feature_number), (1, 0, 2, 3)
    )
    left_blocks = left_blocks.reshape(4, summed_extent, block_rows * first_feature_number)

    def step(carry, pieces):
        grad_tile, left_tile = pieces
        outer_matrix = jnp.einsum("ijp,cep->icje", grad_tile, weight3, precision=exact_arithmetic)
        outer_matrix = outer_matrix.reshape(
            block_rows * first_feature_number, tile_j * second_feature_number
        )
        left_part = (
            jnp.einsum("sk,xk->sx", second_flat, outer_matrix, precision=exact_arithmetic)
            / summed_extent
        )
        carry = (
            carry
            + jnp.einsum("sx,xk->sk", left_tile, outer_matrix, precision=exact_arithmetic)
            / summed_extent
        )
        return (carry, left_part.reshape(summed_extent, block_rows, first_feature_number))

    start_right = jnp.zeros((summed_extent, tile_j * second_feature_number), jnp.float32)
    right_flat, left_parts = lax.scan(step, start_right, (grad_blocks, left_blocks))
    right_part = right_flat.reshape(summed_extent, tile_j, second_feature_number)
    left_part = jnp.transpose(left_parts, (1, 0, 2, 3)).reshape(
        summed_extent, tile_i, first_feature_number
    )
    moved = lax.all_to_all(left_part, "row", split_axis=0, concat_axis=1, tiled=True)
    grad_left = lax.psum_scatter(moved, "col", scatter_dimension=1, tiled=True)
    grad_right = lax.psum_scatter(right_part, "row", scatter_dimension=0, tiled=True)
    return (grad_left, grad_right)


def solution(mesh):
    return jax.shard_map(
        on_device,
        mesh=mesh,
        in_specs=(P("row", "col", None), P("row", "col", None), P("row", "col", None), P()),
        out_specs=(P("row", "col", None), P("row", "col", None)),
        check_vma=False,
    )
```

profile of v0, /device:TPU:0, one launch (start us, length us, event | category | flops | bytes accessed | tf_op | source)
XLA Modules:
  0.0 162.7 jit_solution(6205969470854914557)
XLA Ops:
  8.0 0.8 copy.22
  8.8 32.5 %all_gather.6 = f32[4,128,32]{2,0,1:T(4,128)S(1)} all-gather(f32[4,16,32]{2,0,1:T(4,128)S(1)} %copy.22), channel_id=1, replica_groups=mesh['row'=4,'col'=8] {'col'}, dimensions={1}, use_global_device_ids=true | all-gather | bytes 73728 | tf_op jit(solution)/shard_map/all_gather | solution.py:21
  41.4 0.8 reshape.42
  42.2 3.3 %all-to-all-start = ((f32[4,1,4096]{2,1,0:T(1,128)}), f32[4,1,4096]{2,1,0:T(1,128)S(1)}, u32[]{:S(2)}, u32[]{:S(2)}) async-start(f32[4,1,4096]{2,1,0:T(1,128)} %reshape.42), calls=%async_computation | async-start | bytes 131072 | tf_op jit(solution)/shard_map/all_to_all | solution.py:22
  45.5 5.7 %all_gather.7 = f32[16,16,32]{2,1,0:T(8,128)S(1)} all-gather(f32[4,16,32]{2,1,0:T(8,128)} %param.7), channel_id=1, replica_groups=mesh['row'=4,'col'=8] {'row'}, dimensions={0}, use_global_device_ids=true | all-gather | bytes 40960 | tf_op jit(solution)/shard_map/all_gather | solution.py:19
  51.3 0.5 broadcast.20
  51.8 0.8 reduce
  53.0 21.0 %while.13 = (s32[]{:T(128)}, f32[16,512]{1,0:T(8,128)S(1)}, f32[4,16,8,32]{3,2,0,1:T(8,128)S(1)}, f32[4,16,256]{2,0,1:T(4,128)S(1)}, f32[4,8,16,128]{3,2,1,0:T(8...) while((s32[]{:T(128)}, f32[16,512]{1,0:T(8,128)S(1)}, ...), condition=%wide.region_1.2_spmd.clone, body=%wide.region_0.1_spmd.clone.sunk | while | flops 251686912 | bytes 3539567 | solution.py:49
  53.1 3.4 %convolution_bitcast_fusion.2 = f32[8,32,16,32]{3,2,1,0:T(8,128)S(1)} fusion(f32[32,32,128]{2,1,0:T(8,128)S(1)} %get-tuple-element.180, f32[4,8,16,128]{3,2,1,0:T(8,128)} %get-tuple-element.179, s32[]{:T(128)} %get-tuple-element.166), kind=kOutput, calls=%fused_computation.clone.1 | convolution fusion | flops 201326592 | bytes 1114624 | tf_op jit(solution)/shard_map/while/body/eval_jaxpr/ijp,cep->icje/dot_general | solution.py:33
  56.4 0.8 reshape.47
  57.3 0.4 fusion.21
  57.7 0.5 fusion.22
  58.3 3.4 %convolution_bitcast_fusion.2 = f32[8,32,16,32]{3,2,1,0:T(8,128)S(1)} fusion(f32[32,32,128]{2,1,0:T(8,128)S(1)} %get-tuple-element.180, f32[4,8,16,128]{3,2,1,0:T(8,128)} %get-tuple-element.179, s32[]{:T(128)} %get-tuple-element.166), kind=kOutput, calls=%fused_computation.clone.1 | convolution fusion | flops 201326592 | bytes 1114624 | tf_op jit(solution)/shard_map/while/body/eval_jaxpr/ijp,cep->icje/dot_general | solution.py:33
  61.7 0.8 reshape.47
  62.5 0.4 fusion.21
  62.9 0.5 fusion.22
  63.6 3.4 %convolution_bitcast_fusion.2 = f32[8,32,16,32]{3,2,1,0:T(8,128)S(1)} fusion(f32[32,32,128]{2,1,0:T(8,128)S(1)} %get-tuple-element.180, f32[4,8,16,128]{3,2,1,0:T(8,128)} %get-tuple-element.179, s32[]{:T(128)} %get-tuple-element.166), kind=kOutput, calls=%fused_computation.clone.1 | convolution fusion | flops 201326592 | bytes 1114624 | tf_op jit(solution)/shard_map/while/body/eval_jaxpr/ijp,cep->icje/dot_general | solution.py:33
  66.9 0.8 reshape.47
  67.8 0.4 fusion.21
  68.2 0.5 fusion.22
  68.8 3.4 %convolution_bitcast_fusion.2 = f32[8,32,16,32]{3,2,1,0:T(8,128)S(1)} fusion(f32[32,32,128]{2,1,0:T(8,128)S(1)} %get-tuple-element.180, f32[4,8,16,128]{3,2,1,0:T(8,128)} %get-tuple-element.179, s32[]{:T(128)} %get-tuple-element.166), kind=kOutput, calls=%fused_computation.clone.1 | convolution fusion | flops 201326592 | bytes 1114624 | tf_op jit(solution)/shard_map/while/body/eval_jaxpr/ijp,cep->icje/dot_general | solution.py:33
  72.2 0.8 reshape.47
  73.0 0.4 fusion.21
  73.4 0.5 fusion.22
  74.2 7.1 %all_to_all.33 = f32[4,1,4096]{2,1,0:T(1,128)S(1)} all-to-all(f32[4,1,4096]{2,1,0:T(1,128)S(1)} %reshape.44), channel_id=1, replica_groups=mesh['row'=4,'col'=8] {'row'}, dimensions={0} | all-to-all | bytes 131072 | tf_op jit(solution)/shard_map/all_to_all | solution.py:54
  81.3 0.8 reduce.1
  82.2 0.9 copy.33
  83.2 0.6 dynamic-slice
  84.4 0.7 reshape.37
  85.2 68.7 %all-reduce.3.cloned.1.call-done = f32[4,128,32]{2,0,1:T(4,128)} async-done(((f32[4,128,32]{2,0,1:T(4,128)}), f32[4,128,32]{2,0,1:T(4,128)}) %all-reduce.3.cloned.1.call-update) | async-done | bytes 65552
  153.9 0.8 constant_dynamic-slice_fusion.1
  154.6 0.6 copy.29
  (30 shorter events, 1.3 us)
Async XLA Ops:
  8.0 45.0 %copy-start = (f32[1024,128]{1,0:T(8,128)S(1)}, f32[1024,128]{1,0:T(8,128)}, u32[]{:S(2)}) copy-start(f32[1024,128]{1,0:T(8,128)} %param.9) | copy-start | bytes 1572868
  42.2 9.1 %all-to-all-start = ((f32[4,1,4096]{2,1,0:T(1,128)}), f32[4,1,4096]{2,1,0:T(1,128)S(1)}, u32[]{:S(2)}, u32[]{:S(2)}) async-start(f32[4,1,4096]{2,1,0:T(1,128)} %reshape.42), calls=%async_computation | async-start | bytes 131072 | tf_op jit(solution)/shard_map/all_to_all | solution.py:22
  45.5 108.4 %all-reduce.3.cloned.1.call-start = ((), (), s32[]{:S(2)}) async-start(), calls=%async_computation.4 | async-start | bytes 524288
  53.0 30.2 %copy-start.1 = (u32[32]{0:T(128)S(1)}, u32[32]{0:T(128)}, u32[]{:S(2)}) copy-start(u32[32]{0:T(128)} %constant.23) | copy-start | bytes 388
  83.1 72.1 %reduce-scatter.2.cloned.1.call-start = ((), (), s32[]{:S(2)}) async-start(), calls=%async_computation.3 | async-start | bytes 163840 | tf_op jit(solution)/shard_map/reduce_scatter | solution.py:56
Sparse Core Ops, SparseCore 0:
  83.2 70.5 all-reduce.2
Sparse Core Ops, SparseCore 1:
  86.7 19.6 reduce-scatter.1
where the time goes:
time: 163 us
  waiting for transfers between devices  68.7 us (42%)
  blocking collectives  45.3 us (28%)
  matrix products  17 us (10%)
  between operations  16.2 us (10%)
  local copies, waits for them, and re-layouts  10.3 us (6%)
  starting transfers between devices  3.37 us (2%)
    unnamed x3, waiting for transfers between devices  68.7 us
    all_gather x1, blocking collectives, on_device(): lax.all_gather(first_alignment_matrix, 'col', axis=1, tiled=True)  32.5 us
    dot_general x4, matrix products, step(): jnp.einsum('ijp,cep->icje', grad_tile, weight3, precision=exact_arithmetic)  13.5 us
    all_to_all x1, blocking collectives, on_device(): lax.all_to_all(left_part, 'row', split_axis=0, concat_axis=1, tiled=True)  7.07 us
    all_gather x1, blocking collectives, on_device(): lax.all_gather(second_alignment_matrix, 'row', axis=0, tiled=True)  5.67 us
    unnamed x12, local copies, waits for them, and re-layouts  4.09 us
    reshape x4, local copies, waits for them, and re-layouts, step(): outer_matrix.reshape(block_rows * first_feature_number, tile_j * second_f...  3.31 us
    all_to_all x1, starting transfers between devices, on_device(): lax.all_to_all(expanded_outer_term, 'row', split_axis=1, concat_axis=0, t...  3.28 us
  transfers between devices with their start and end apart: 3, of which 1 were waited for; matrix products, arithmetic and copies ran while one was open for 2% of the time, Pallas kernels for 0%

commit v1 on v0

v1 whole, which is shorter than its diff:
```python
import functools

import jax
import jax.numpy as jnp
from jax import lax
from jax.experimental import pallas as pl
from jax.experimental.pallas import tpu as pltpu
from jax.sharding import PartitionSpec as P

MESH = pl.DeviceIdType.MESH
WIDE = 256
LANES = 128


def split(x):
    high = x.astype(jnp.bfloat16)
    low = (x - high.astype(jnp.float32)).astype(jnp.bfloat16)
    return high, low


def dot_nt(x, y):
    return lax.dot_general(x, y, (((1,), (1,)), ((), ())), preferred_element_type=jnp.float32)


def kernel(
    rows, cols,
    a_ref, b_ref, d_hbm, w_hbm, left_ref, right_ref,
    a_all, b_all, d_buf, w_buf, a_high, a_low, b_high, b_low,
    g_high, g_low, h_high, h_low,
    left_send, right_send, left_recv, right_recv, turned,
    local_sem, a_send_sem, a_recv_sem, b_send_sem, b_recv_sem,
    l_send_sem, l_recv_sem, r_send_sem, r_recv_sem,
):
    seqs, res, feats = a_ref.shape
    feats_e = b_ref.shape[2]
    tile_j = res
    tile_i = d_hbm.shape[0] // tile_j
    halves = tile_i // res
    total = seqs * rows
    group_c = WIDE // feats_e
    group_e = WIDE // feats
    chunks_c = feats // group_c
    chunks_e = feats_e // group_e
    piece_l = seqs * group_c
    piece_r = seqs * group_e

    r = lax.axis_index("row")
    q = lax.axis_index("col")
    owner_row = q // halves
    part = q % halves
    inside = owner_row == r

    copy_d = pltpu.make_async_copy(d_hbm, d_buf, local_sem.at[0])
    copy_w = pltpu.make_async_copy(w_hbm, w_buf, local_sem.at[1])
    copy_d.start()
    copy_w.start()

    barrier = pltpu.get_barrier_semaphore()

    def signal(row, col):
        pl.semaphore_signal(barrier, inc=1, device_id=(row, col), device_id_type=MESH)

    def unless_self(row, col, act, mine=None):
        same = jnp.logical_and(row == r, col == q)
        pl.when(jnp.logical_not(same))(act)
        if mine is not None:
            pl.when(same)(mine)

    for k in range(cols):
        unless_self(owner_row, k, functools.partial(signal, owner_row, k))
    for k in range(rows):
        for h in range(halves):
            col = r * halves + h
            unless_self(k, col, functools.partial(signal, k, col))
    for step in range(1, rows):
        signal((r + step) % rows, q)

    b_all[r] = b_ref[...]

    @pl.when(inside)
    def _():
        a_all[part, r] = a_ref[...]

    pl.semaphore_wait(barrier, (rows - 1) + 2 * jnp.where(inside, cols - 1, cols))

    def copy_b(step):
        dest = (r + step) % rows
        return pltpu.make_async_remote_copy(
            src_ref=b_ref, dst_ref=b_all.at[r], send_sem=b_send_sem.at[step],
            recv_sem=b_recv_sem.at[r], device_id=(dest, q), device_id_type=MESH)

    def copy_a(k):
        return pltpu.make_async_remote_copy(
            src_ref=a_ref, dst_ref=a_all.at[part, r], send_sem=a_send_sem.at[k],
            recv_sem=a_recv_sem.at[part, r], device_id=(owner_row, k), device_id_type=MESH)

    for step in range(1, rows):
        copy_b(step).start()
    for k in range(cols):
        unless_self(owner_row, k, lambda k=k: copy_a(k).start())

    copy_d.wait()
    copy_w.wait()
    d_plain = d_buf[...]
    d_turned = jnp.concatenate(
        [d_buf[pl.ds(j, tile_i, stride=tile_j), :] for j in range(tile_j)], axis=0)

    def expand(d, w, high_ref, low_ref, chunks):
        d_high, d_low = split(d)
        d_both = jnp.concatenate([d_high, d_low], axis=1)
        for n in range(chunks):
            w_high, w_low = split(w[n])
            out = dot_nt(d_both, jnp.concatenate([w_high, w_high], axis=1))
            out = out + dot_nt(d_high, w_low)
            out_high, out_low = split(out)
            high_ref[n] = out_high
            low_ref[n] = out_low

    expand(d_turned, [w_buf[n * WIDE:(n + 1) * WIDE, :] for n in range(chunks_c)],
           g_high, g_low, chunks_c)
    expand(d_plain, [jnp.concatenate(
        [w_buf[pl.ds(n * group_e + e, feats, stride=feats_e), :] for e in range(group_e)], axis=0)
        for n in range(chunks_e)], h_high, h_low, chunks_e)

    def repeat_lanes(x, high_ref, low_ref):
        width = x.shape[1]
        place = lax.broadcasted_iota(jnp.int32, (width, LANES), 1) % width
        unit = (place == lax.broadcasted_iota(jnp.int32, (width, LANES), 0)).astype(jnp.bfloat16)
        high, low = split(x)
        high_ref[...] = jnp.dot(high, unit, preferred_element_type=jnp.float32)
        low_ref[...] = jnp.dot(low, unit, preferred_element_type=jnp.float32)

    def spread(ref, start, stride, group, width):
        x = ref[pl.ds(start, total, stride=stride), :]
        x = jnp.concatenate([x] * (WIDE // LANES), axis=1)
        lane = lax.broadcasted_iota(jnp.int32, (1, group, WIDE), 2) // width
        keep = lane == lax.broadcasted_iota(jnp.int32, (1, group, WIDE), 1)
        x = jnp.where(keep, x[:, None, :], 0.0)
        return x.reshape(total * group, WIDE).astype(jnp.bfloat16)

    def contract(coef_high, coef_low, mat_high, mat_low):
        size = coef_high.shape[0]
        both = dot_nt(jnp.concatenate([coef_high, coef_low], axis=0), mat_high)
        return both[:size] + both[size:] + dot_nt(coef_high, mat_low)

    for step in range(1, rows):
        source = (r + step) % rows
        pltpu.make_async_remote_copy(
            src_ref=b_ref, dst_ref=b_all.at[source], send_sem=b_send_sem.at[step],
            recv_sem=b_recv_sem.at[source], device_id=(source, q), device_id_type=MESH).wait_recv()
    repeat_lanes(b_all[...].reshape(total * tile_j, feats_e), b_high, b_low)
    sum_left = None
    for j in range(tile_j):
        span = slice(j * tile_i, (j + 1) * tile_i)
        term = contract(
            spread(b_high, j, tile_j, group_c, feats_e),
            spread(b_low, j, tile_j, group_c, feats_e),
            jnp.concatenate([g_high[n, span, :] for n in range(chunks_c)], axis=0),
            jnp.concatenate([g_low[n, span, :] for n in range(chunks_c)], axis=0))
        sum_left = term if sum_left is None else sum_left + term
    left_send[...] = sum_left.reshape(rows, piece_l, chunks_c * tile_i)

    def copy_l(k, h):
        return pltpu.make_async_remote_copy(
            src_ref=left_send.at[k], dst_ref=left_recv.at[q], send_sem=l_send_sem.at[k, h],
            recv_sem=l_recv_sem.at[q], device_id=(k, r * halves + h), device_id_type=MESH)

    for k in range(rows):
        for h in range(halves):
            def mine(k=k):
                left_recv[q] = left_send[k]

            unless_self(k, r * halves + h, lambda k=k, h=h: copy_l(k, h).start(), mine)

    for k in range(rows):
        for h in range(halves):
            def arrive(k=k, h=h):
                pltpu.make_async_remote_copy(
                    src_ref=a_ref, dst_ref=a_all.at[h, k], send_sem=a_send_sem.at[0],
                    recv_sem=a_recv_sem.at[h, k], device_id=(k, r * halves + h),
                    device_id_type=MESH).wait_recv()

            unless_self(k, r * halves + h, arrive)
    repeat_lanes(a_all[...].reshape(total * tile_i, feats), a_high, a_low)
    sum_right = None
    for i in range(tile_i):
        span = slice(i * tile_j, (i + 1) * tile_j)
        start = (i // res) * total * res + i % res
        term = contract(
            spread(a_high, start, res, group_e, feats),
            spread(a_low, start, res, group_e, feats),
            jnp.concatenate([h_high[n, span, :] for n in range(chunks_e)], axis=0),
            jnp.concatenate([h_low[n, span, :] for n in range(chunks_e)], axis=0))
        sum_right = term if sum_right is None else sum_right + term
    right_send[...] = sum_right.reshape(rows, piece_r, chunks_e * tile_j)
    right_recv[r] = right_send[r]

    def copy_r(step):
        dest = (r + step) % rows
        return pltpu.make_async_remote_copy(
            src_ref=right_send.at[dest], dst_ref=right_recv.at[r], send_sem=r_send_sem.at[step],
            recv_sem=r_recv_sem.at[r], device_id=(dest, q), device_id_type=MESH)

    for step in range(1, rows):
        copy_r(step).start()

    for k in range(cols):
        def arrive(k=k):
            pltpu.make_async_remote_copy(
                src_ref=left_send.at[0], dst_ref=left_recv.at[k], send_sem=l_send_sem.at[0, 0],
                recv_sem=l_recv_sem.at[k], device_id=(owner_row, k),
                device_id_type=MESH).wait_recv()

        unless_self(owner_row, k, arrive)
    done = jnp.sum(left_recv[...], axis=0) / total
    turned[...] = done.T
    for n in range(chunks_c):
        rows_n = turned[pl.ds(n * tile_i + part * res, res), :]
        for s in range(seqs):
            left_ref[s, :, n * group_c:(n + 1) * group_c] = rows_n[:, s * group_c:(s + 1) * group_c]

    for step in range(1, rows):
        source = (r + step) % rows
        pltpu.make_async_remote_copy(
            src_ref=right_send.at[source], dst_ref=right_recv.at[source],
            send_sem=r_send_sem.at[step], recv_sem=r_recv_sem.at[source],
            device_id=(source, q), device_id_type=MESH).wait_recv()
    done = (jnp.sum(right_recv[...], axis=0) / total).T
    for n in range(chunks_e):
        for s in range(seqs):
            right_ref[s, :, n * group_e:(n + 1) * group_e] = done[
                n * tile_j:(n + 1) * tile_j, s * group_e:(s + 1) * group_e]

    for step in range(1, rows):
        copy_b(step).wait_send()
        copy_r(step).wait_send()
    for k in range(cols):
        unless_self(owner_row, k, lambda k=k: copy_a(k).wait_send())
    for k in range(rows):
        for h in range(halves):
            unless_self(k, r * halves + h, lambda k=k, h=h: copy_l(k, h).wait_send())


def on_device(rows, cols, a, b, d, w):
    seqs, res, feats = a.shape
    feats_e = b.shape[2]
    tile_i, tile_j, pair = d.shape
    halves = tile_i // res
    total = seqs * rows
    group_c, group_e = WIDE // feats_e, WIDE // feats
    chunks_c, chunks_e = feats // group_c, feats_e // group_e
    pairs = tile_i * tile_j
    vmem = pl.BlockSpec(memory_space=pltpu.VMEM)
    anywhere = pl.BlockSpec(memory_space=pl.ANY)
    f32, bf16 = jnp.float32, jnp.bfloat16
    left_piece = (seqs * group_c, chunks_c * tile_i)
    right_piece = (seqs * group_e, chunks_e * tile_j)
    dma = pltpu.SemaphoreType.DMA
    return pl.pallas_call(
        functools.partial(kernel, rows, cols),
        out_shape=(jax.ShapeDtypeStruct(a.shape, f32), jax.ShapeDtypeStruct(b.shape, f32)),
        in_specs=[vmem, vmem, anywhere, anywhere],
        out_specs=(vmem, vmem),
        scratch_shapes=[
            pltpu.VMEM((halves, rows) + a.shape, f32),
            pltpu.VMEM((rows,) + b.shape, f32),
            pltpu.VMEM((pairs, pair), f32),
            pltpu.VMEM(w.shape, f32),
            pltpu.VMEM((total * tile_i, LANES), f32),
            pltpu.VMEM((total * tile_i, LANES), f32),
            pltpu.VMEM((total * tile_j, LANES), f32),
            pltpu.VMEM((total * tile_j, LANES), f32),
            pltpu.VMEM((chunks_c, pairs, WIDE), bf16),
            pltpu.VMEM((chunks_c, pairs, WIDE), bf16),
            pltpu.VMEM((chunks_e, pairs, WIDE), bf16),
            pltpu.VMEM((chunks_e, pairs, WIDE), bf16),
            pltpu.VMEM((rows,) + left_piece, f32),
            pltpu.VMEM((rows,) + right_piece, f32),
            pltpu.VMEM((cols,) + left_piece, f32),
            pltpu.VMEM((rows,) + right_piece, f32),
            pltpu.VMEM(left_piece[::-1], f32),
            dma((2,)),
            dma((cols,)),
            dma((halves, rows)),
            dma((rows,)),
            dma((rows,)),
            dma((rows, halves)),
            dma((cols,)),
            dma((rows,)),
            dma((rows,)),
        ],
        compiler_params=pltpu.CompilerParams(
            collective_id=0, has_side_effects=True, vmem_limit_bytes=32 * 2**20),
    )(a, b, d.reshape(pairs, pair), w)


def solution(mesh):
    spec = P("row", "col", None)
    return jax.shard_map(
        functools.partial(on_device, mesh.shape["row"], mesh.shape["col"]),
        mesh=mesh,
        in_specs=(spec, spec, spec, P()),
        out_specs=(spec, spec),
        check_vma=False,
    )
```

time: 163 us -> 27.8 us (0.17)
  the two profiles are of different devices: /device:TPU:0 before, /device:TPU:13 now
where the time goes in v1:
time: 27.8 us; the launch traced here: 27.4 us
  Pallas kernels  22.1 us (79%)
  local copies, waits for them, and re-layouts  4.73 us (17%)
  between operations  0.65 us (2%)
    pallas_call x1, Pallas kernels, on_device(): pl.pallas_call(functools.partial(kernel, rows, cols), out_shape=(jax.Shap...  22.1 us
    unnamed x10, local copies, waits for them, and re-layouts  4.73 us

profile of v1, /device:TPU:13, one launch (start us, length us, event | category | flops | bytes accessed | tf_op | source)
XLA Modules:
  0.0 27.4 jit_solution(7843521397659747514)
XLA Ops:
  0.6 0.0 copy-start
  0.6 1.0 %copy-done = f32[1024,128]{1,0:T(8,128)S(1)} copy-done((f32[1024,128]{1,0:T(8,128)S(1)}, f32[1024,128]{1,0:T(8,128)}, u32[]{:S(2)}) %copy-start) | copy-done | bytes 524312
  1.7 0.0 copy-start.1
  1.7 0.9 %copy-done.1 = f32[32,16,128]{2,1,0:T(8,128)S(1)} copy-done((f32[32,16,128]{2,1,0:T(8,128)S(1)}, f32[32,16,128]{2,1,0:T(8,128)}, u32[]{:S(2)}) %copy-start.1) | copy-done | bytes 262168
  2.6 0.0 copy-start.2
  2.6 0.8 %copy-done.2 = f32[4,16,32]{2,1,0:T(8,128)S(1)} copy-done((f32[4,16,32]{2,1,0:T(8,128)S(1)}, f32[4,16,32]{2,1,0:T(8,128)}, u32[]{:S(2)}) %copy-start.2) | copy-done | bytes 8216
  3.4 0.0 copy-start.3
  3.4 0.8 %copy-done.3 = f32[4,16,32]{2,1,0:T(8,128)S(1)} copy-done((f32[4,16,32]{2,1,0:T(8,128)S(1)}, f32[4,16,32]{2,1,0:T(8,128)}, u32[]{:S(2)}) %copy-start.3) | copy-done | bytes 8216
  4.1 22.1 %shard_map.59 = (f32[4,16,32]{2,1,0:T(8,128)S(1)}, f32[4,16,32]{2,1,0:T(8,128)S(1)}) custom-call(f32[4,16,32]{2,1,0:T(8,128)S(1)} %copy-done.2, f32[4,16,32]{2,1,0:T(8,128)S(1)} %copy-done.3, f32[512,128]{1,0:T(8,128)S(1)} %bitcast.1, f32[1024,128]{1,0:T(8,128)S(1)} %copy-done), custom_call_target="tpu_custom_call" | custom-call | tf_op jit(solution)/shard_map/pallas_call | solution.py:259
  26.2 0.6 %copy.8 = f32[4,16,32]{2,1,0:T(8,128)} copy(f32[4,16,32]{2,1,0:T(8,128)S(1)} %get-tuple-element.4) | data formatting | bytes 16384
  26.8 0.6 %copy.9 = f32[4,16,32]{2,1,0:T(8,128)} copy(f32[4,16,32]{2,1,0:T(8,128)S(1)} %get-tuple-element.5) | data formatting | bytes 16384
Async XLA Ops:
  0.6 1.0 %copy-start = (f32[1024,128]{1,0:T(8,128)S(1)}, f32[1024,128]{1,0:T(8,128)}, u32[]{:S(2)}) copy-start(f32[1024,128]{1,0:T(8,128)} %w_hbm.1) | copy-start | bytes 1572868
  1.7 0.9 %copy-start.1 = (f32[32,16,128]{2,1,0:T(8,128)S(1)}, f32[32,16,128]{2,1,0:T(8,128)}, u32[]{:S(2)}) copy-start(f32[32,16,128]{2,1,0:T(8,128)} %param.6) | copy-start | bytes 786436
  2.6 0.8 %copy-start.2 = (f32[4,16,32]{2,1,0:T(8,128)S(1)}, f32[4,16,32]{2,1,0:T(8,128)}, u32[]{:S(2)}) copy-start(f32[4,16,32]{2,1,0:T(8,128)} %a_ref.1) | copy-start | bytes 24580
  3.4 0.8 %copy-start.3 = (f32[4,16,32]{2,1,0:T(8,128)S(1)}, f32[4,16,32]{2,1,0:T(8,128)}, u32[]{:S(2)}) copy-start(f32[4,16,32]{2,1,0:T(8,128)} %b_ref.1) | copy-start | bytes 24580

commit v2 on v1

v2 whole, which is shorter than its diff:
```python
import functools

import jax
import jax.numpy as jnp
from jax import lax
from jax.experimental import pallas as pl
from jax.experimental.pallas import tpu as pltpu
from jax.sharding import PartitionSpec as P

MESH = pl.DeviceIdType.MESH
WIDE = 256
LANES = 128
DEPTH = 4


def split(x):
    high = x.astype(jnp.bfloat16)
    low = (x - high.astype(jnp.float32)).astype(jnp.bfloat16)
    return high, low


def dot_nt(x, y):
    return lax.dot_general(x, y, (((1,), (1,)), ((), ())), preferred_element_type=jnp.float32)


def kernel(
    rows, cols,
    a_hbm, b_hbm, d_hbm, w_hbm, left_ref, right_ref,
    a_own, b_own, a_pack, b_pack, a_all, b_all, d_buf, w_buf, a_high, a_low, b_high, b_low,
    g_high, g_low, h_high, h_low,
    left_sum, right_sum, left_send, right_send, left_recv, right_recv,
    local_sem, a_send_sem, a_recv_sem, b_send_sem, b_recv_sem,
    l_send_sem, l_recv_sem, r_send_sem, r_recv_sem,
):
    seqs, res, feats = a_hbm.shape
    feats_e = b_hbm.shape[2]
    tile_j = res
    tile_i = d_hbm.shape[0] // tile_j
    halves = tile_i // res
    total = seqs * rows
    group_c = WIDE // feats_e
    group_e = WIDE // feats
    chunks_c = feats // group_c
    chunks_e = feats_e // group_e

    r = lax.axis_index("row")
    q = lax.axis_index("col")
    owner_row = q // halves
    part = q % halves
    inside = owner_row == r

    copy_d = pltpu.make_async_copy(d_hbm, d_buf, local_sem.at[0])
    copy_w = pltpu.make_async_copy(w_hbm, w_buf, local_sem.at[1])
    fetch_a = pltpu.make_async_copy(a_hbm, a_own, local_sem.at[2])
    fetch_b = pltpu.make_async_copy(b_hbm, b_own, local_sem.at[3])
    fetch_b.start()
    fetch_a.start()
    copy_d.start()
    copy_w.start()

    barrier = pltpu.get_barrier_semaphore()

    def signal(row, col):
        pl.semaphore_signal(barrier, inc=1, device_id=(row, col), device_id_type=MESH)

    def unless_self(row, col, act, mine=None):
        same = jnp.logical_and(row == r, col == q)
        pl.when(jnp.logical_not(same))(act)
        if mine is not None:
            pl.when(same)(mine)

    for k in range(cols):
        unless_self(owner_row, k, functools.partial(signal, owner_row, k))
    for k in range(rows):
        for h in range(halves):
            col = r * halves + h
            unless_self(k, col, functools.partial(signal, k, col))
    for step in range(1, rows):
        signal((r + step) % rows, q)

    fetch_b.wait()
    b_pack[...] = jnp.concatenate([b_own[s] for s in range(seqs)], axis=1)
    b_all[r] = b_pack[...]
    fetch_a.wait()
    a_pack[...] = jnp.concatenate([a_own[s] for s in range(seqs)], axis=1)

    @pl.when(inside)
    def _():
        a_all[part, r] = a_pack[...]

    pl.semaphore_wait(barrier, (rows - 1) + 2 * jnp.where(inside, cols - 1, cols))

    def copy_b(step):
        dest = (r + step) % rows
        return pltpu.make_async_remote_copy(
            src_ref=b_pack, dst_ref=b_all.at[r], send_sem=b_send_sem.at[step],
            recv_sem=b_recv_sem.at[r], device_id=(dest, q), device_id_type=MESH)

    def copy_a(k):
        return pltpu.make_async_remote_copy(
            src_ref=a_pack, dst_ref=a_all.at[part, r], send_sem=a_send_sem.at[k],
            recv_sem=a_recv_sem.at[part, r], device_id=(owner_row, k), device_id_type=MESH)

    for step in range(1, rows):
        copy_b(step).start()
    for k in range(cols):
        unless_self(owner_row, k, lambda k=k: copy_a(k).start())

    copy_d.wait()
    copy_w.wait()
    d_plain = d_buf[...]
    d_turned = jnp.concatenate(
        [d_buf[pl.ds(j, tile_i, stride=tile_j), :] for j in range(tile_j)], axis=0)

    def expand(d, w, high_ref, low_ref, chunks):
        d_high, d_low = split(d)
        d_both = jnp.concatenate([d_high, d_low], axis=1)
        for n in range(chunks):
            w_high, w_low = split(w[n])
            out = dot_nt(d_both, jnp.concatenate([w_high, w_high], axis=1))
            out = out + dot_nt(d_high, w_low)
            out_high, out_low = split(out)
            high_ref[n] = out_high
            low_ref[n] = out_low

    expand(d_turned, [w_buf[n * WIDE:(n + 1) * WIDE, :] for n in range(chunks_c)],
           g_high, g_low, chunks_c)
    expand(d_plain, [jnp.concatenate(
        [w_buf[pl.ds(n * group_e + e, feats, stride=feats_e), :] for e in range(group_e)], axis=0)
        for n in range(chunks_e)], h_high, h_low, chunks_e)

    def repeat_lanes(x, width, high_ref, low_ref, base):
        size = x.shape[0]
        source = lax.broadcasted_iota(jnp.int32, (LANES, seqs * LANES), 0)
        target = lax.broadcasted_iota(jnp.int32, (LANES, seqs * LANES), 1)
        unit = (source == target // LANES * width + target % width).astype(jnp.bfloat16)
        for part_of, ref in zip(split(x), (high_ref, low_ref)):
            out = jnp.dot(part_of, unit, preferred_element_type=jnp.float32)
            for s in range(seqs):
                ref[base + s * size:base + (s + 1) * size, :] = out[:, s * LANES:(s + 1) * LANES]

    def masks(group, width):
        lane = lax.broadcasted_iota(jnp.int32, (group, WIDE), 1) // width
        block = lax.broadcasted_iota(jnp.int32, (group, WIDE), 0)
        return (lane == block).astype(jnp.float32).astype(jnp.bfloat16)

    def spread(ref, start, mask):
        x = ref[pl.ds(start, total, stride=res), :].astype(jnp.bfloat16)
        x = jnp.concatenate([x] * (WIDE // LANES), axis=1)
        return jnp.concatenate([x * mask[k:k + 1] for k in range(mask.shape[0])], axis=0)

    def contract(count, coef, mat):
        acc = None
        for first in range(0, count, DEPTH):
            steps = range(first, min(first + DEPTH, count))
            lhs = jnp.concatenate([coef(n) for n in steps], axis=1)
            rhs = jnp.concatenate([mat(n) for n in steps], axis=1)
            term = dot_nt(lhs, rhs)
            acc = term if acc is None else acc + term
        size, width = acc.shape[0] // 2, acc.shape[1] // 2
        return acc[:size, :width] + acc[:size, width:] + acc[size:, :width]

    def pieces(ref, k, group, parts, width):
        fold = LANES // width
        x = [ref[pl.ds(s * rows + k, group, stride=total), :] for s in range(seqs)]
        each = seqs // fold
        x = [jnp.concatenate(x[u * each:(u + 1) * each], axis=0) for u in range(fold)]
        return [jnp.concatenate([y[:, h * width:(h + 1) * width] for y in x], axis=1)
                for h in range(parts)]

    for step in range(1, rows):
        source = (r + step) % rows
        pltpu.make_async_remote_copy(
            src_ref=b_pack, dst_ref=b_all.at[source], send_sem=b_send_sem.at[step],
            recv_sem=b_recv_sem.at[source], device_id=(source, q), device_id_type=MESH).wait_recv()
    repeat_lanes(b_all[...].reshape(rows * res, LANES), feats_e, b_high, b_low, 0)
    mask_c = masks(group_c, feats_e)

    def left_coef(j):
        return jnp.concatenate([spread(b_high, j, mask_c), spread(b_low, j, mask_c)], axis=0)

    def left_mat(j):
        return jnp.concatenate(
            [ref[n, j * tile_i + h * res:j * tile_i + (h + 1) * res, :]
             for ref in (g_high, g_low) for h in range(halves) for n in range(chunks_c)], axis=0)

    left_sum[...] = contract(tile_j, left_coef, left_mat)
    for k in range(rows):
        for h, piece in enumerate(pieces(left_sum, k, group_c, halves, chunks_c * res)):
            left_send[k, h] = piece

    def copy_l(k, h):
        return pltpu.make_async_remote_copy(
            src_ref=left_send.at[k, h], dst_ref=left_recv.at[q], send_sem=l_send_sem.at[k, h],
            recv_sem=l_recv_sem.at[q], device_id=(k, r * halves + h), device_id_type=MESH)

    for k in range(rows):
        for h in range(halves):
            def mine(k=k, h=h):
                left_recv[q] = left_send[k, h]

            unless_self(k, r * halves + h, lambda k=k, h=h: copy_l(k, h).start(), mine)

    for k in range(rows):
        for h in range(halves):
            def arrive(k=k, h=h):
                pltpu.make_async_remote_copy(
                    src_ref=a_pack, dst_ref=a_all.at[h, k], send_sem=a_send_sem.at[0],
                    recv_sem=a_recv_sem.at[h, k], device_id=(k, r * halves + h),
                    device_id_type=MESH).wait_recv()

            unless_self(k, r * halves + h, arrive)
    for h in range(halves):
        repeat_lanes(a_all[h].reshape(rows * res, LANES), feats, a_high, a_low, h * total * res)
    mask_e = masks(group_e, feats)

    def right_coef(i):
        start = (i // res) * total * res + i % res
        return jnp.concatenate([spread(a_high, start, mask_e), spread(a_low, start, mask_e)], axis=0)

    def right_mat(i):
        span = slice(i * tile_j, (i + 1) * tile_j)
        return jnp.concatenate(
            [ref[n, span, :] for ref in (h_high, h_low) for n in range(chunks_e)], axis=0)

    right = contract(tile_i, right_coef, right_mat)
    right_sum[...] = jnp.concatenate([right] * (LANES // right.shape[1]), axis=1)
    for k in range(rows):
        right_send[k] = pieces(right_sum, k, group_e, 1, chunks_e * tile_j)[0]
    right_recv[r] = right_send[r]

    def copy_r(step):
        dest = (r + step) % rows
        return pltpu.make_async_remote_copy(
            src_ref=right_send.at[dest], dst_ref=right_recv.at[r], send_sem=r_send_sem.at[step],
            recv_sem=r_recv_sem.at[r], device_id=(dest, q), device_id_type=MESH)

    for step in range(1, rows):
        copy_r(step).start()

    for k in range(cols):
        def arrive(k=k):
            pltpu.make_async_remote_copy(
                src_ref=left_send.at[0, 0], dst_ref=left_recv.at[k], send_sem=l_send_sem.at[0, 0],
                recv_sem=l_recv_sem.at[k], device_id=(owner_row, k),
                device_id_type=MESH).wait_recv()

        unless_self(owner_row, k, arrive)
    left_ref[...] = jnp.sum(left_recv[...], axis=0) / total

    for step in range(1, rows):
        source = (r + step) % rows
        pltpu.make_async_remote_copy(
            src_ref=right_send.at[source], dst_ref=right_recv.at[source],
            send_sem=r_send_sem.at[step], recv_sem=r_recv_sem.at[source],
            device_id=(source, q), device_id_type=MESH).wait_recv()
    right_ref[...] = jnp.sum(right_recv[...], axis=0) / total

    for step in range(1, rows):
        copy_b(step).wait_send()
        copy_r(step).wait_send()
    for k in range(cols):
        unless_self(owner_row, k, lambda k=k: copy_a(k).wait_send())
    for k in range(rows):
        for h in range(halves):
            unless_self(k, r * halves + h, lambda k=k, h=h: copy_l(k, h).wait_send())


def unfold(group_c, group_e, left_ref, right_ref, left_out, right_out):
    for group, ref, out in ((group_c, left_ref, left_out), (group_e, right_ref, right_out)):
        seqs, res, feats = out.shape
        x = ref[...].T
        each = ref.shape[0] // group
        chunks = feats // group
        for s in range(seqs):
            u, v = s // each, s % each
            out[s] = jnp.concatenate(
                [x[(u * chunks + n) * res:(u * chunks + n + 1) * res, v * group:(v + 1) * group]
                 for n in range(chunks)], axis=1)


def on_device(rows, cols, a, b, d, w):
    seqs, res, feats = a.shape
    feats_e = b.shape[2]
    tile_i, tile_j, pair = d.shape
    halves = tile_i // res
    total = seqs * rows
    group_c, group_e = WIDE // feats_e, WIDE // feats
    chunks_c, chunks_e = feats // group_c, feats_e // group_e
    pairs = tile_i * tile_j
    vmem = pl.BlockSpec(memory_space=pltpu.VMEM)
    hbm = pl.BlockSpec(memory_space=pltpu.HBM)
    f32, bf16 = jnp.float32, jnp.bfloat16
    left_piece = (seqs * feats * res // LANES, LANES)
    right_piece = (seqs * feats_e * res // LANES, LANES)
    dma = pltpu.SemaphoreType.DMA
    left, right = pl.pallas_call(
        functools.partial(kernel, rows, cols),
        out_shape=(jax.ShapeDtypeStruct(left_piece, f32), jax.ShapeDtypeStruct(right_piece, f32)),
        in_specs=[hbm] * 4,
        out_specs=(vmem, vmem),
        scratch_shapes=[
            pltpu.VMEM(a.shape, f32),
            pltpu.VMEM(b.shape, f32),
            pltpu.VMEM((res, LANES), f32),
            pltpu.VMEM((res, LANES), f32),
            pltpu.VMEM((halves, rows, res, LANES), f32),
            pltpu.VMEM((rows, res, LANES), f32),
            pltpu.VMEM((pairs, pair), f32),
            pltpu.VMEM(w.shape, f32),
            pltpu.VMEM((total * tile_i, LANES), f32),
            pltpu.VMEM((total * tile_i, LANES), f32),
            pltpu.VMEM((total * tile_j, LANES), f32),
            pltpu.VMEM((total * tile_j, LANES), f32),
            pltpu.VMEM((chunks_c, pairs, WIDE), bf16),
            pltpu.VMEM((chunks_c, pairs, WIDE), bf16),
            pltpu.VMEM((chunks_e, pairs, WIDE), bf16),
            pltpu.VMEM((chunks_e, pairs, WIDE), bf16),
            pltpu.VMEM((total * group_c, LANES), f32),
            pltpu.VMEM((total * group_e, LANES), f32),
            pltpu.VMEM((rows, halves) + left_piece, f32),
            pltpu.VMEM((rows,) + right_piece, f32),
            pltpu.VMEM((cols,) + left_piece, f32),
            pltpu.VMEM((rows,) + right_piece, f32),
            dma((4,)),
            dma((cols,)),
            dma((halves, rows)),
            dma((rows,)),
            dma((rows,)),
            dma((rows, halves)),
            dma((cols,)),
            dma((rows,)),
            dma((rows,)),
        ],
        compiler_params=pltpu.CompilerParams(
            collective_id=0, has_side_effects=True, vmem_limit_bytes=54 * 2**20 - 101 * 2**10),
    )(a, b, d.reshape(pairs, pair), w)
    return pl.pallas_call(
        functools.partial(unfold, group_c, group_e),
        out_shape=(jax.ShapeDtypeStruct(a.shape, f32), jax.ShapeDtypeStruct(b.shape, f32)),
        in_specs=[vmem] * 2,
        out_specs=(vmem, vmem),
    )(left, right)


def solution(mesh):
    spec = P("row", "col", None)
    return jax.shard_map(
        functools.partial(on_device, mesh.shape["row"], mesh.shape["col"]),
        mesh=mesh,
        in_specs=(spec, spec, spec, P()),
        out_specs=(spec, spec),
        check_vma=False,
    )
```

time: 27.8 us -> 19.8 us (0.71)
  the two profiles are of different devices: /device:TPU:13 before, /device:TPU:0 now
where the time goes in v2:
time: 19.8 us; the launch traced here: 19.6 us
  Pallas kernels  17.7 us (89%)
  local copies, waits for them, and re-layouts  1.18 us (6%)
  between operations  0.65 us (3%)
    pallas_call x1, Pallas kernels, on_device(): pl.pallas_call(functools.partial(kernel, rows, cols), out_shape=(jax.Shap...  16.2 us
    pallas_call x1, Pallas kernels, on_device(): pl.pallas_call(functools.partial(unfold, group_c, group_e), out_shape=(ja...  1.54 us
    unnamed x4, local copies, waits for them, and re-layouts  1.18 us

profile of v2, /device:TPU:0, one launch (start us, length us, event | category | flops | bytes accessed | tf_op | source)
XLA Modules:
  0.0 19.6 jit_solution(16586746589711604362)
XLA Ops:
  0.6 16.2 %shard_map.59 = (f32[16,128]{1,0:T(8,128)S(1)}, f32[16,128]{1,0:T(8,128)S(1)}) custom-call(f32[4,16,32]{2,1,0:T(8,128)} %a_hbm.1, f32[4,16,32]{2,1,0:T(8,128)} %b_hbm.1, f32[512,128]{1,0:T(8,128)} %bitcast.1, f32[1024,128]{1,0:T(8,128)} %w_hbm.1), custom_call_target="tpu_custom_call" | custom-call | tf_op jit(solution)/shard_map/pallas_call | solution.py:297
  16.8 0.0 copy-start
  16.8 0.6 %copy-done = f32[16,128]{1,0:T(8,128)} copy-done((f32[16,128]{1,0:T(8,128)}, f32[16,128]{1,0:T(8,128)S(1)}, u32[]{:S(2)}) %copy-start) | copy-done | bytes 8216
  17.4 0.0 copy-start.1
  17.4 0.6 %copy-done.1 = f32[16,128]{1,0:T(8,128)} copy-done((f32[16,128]{1,0:T(8,128)}, f32[16,128]{1,0:T(8,128)S(1)}, u32[]{:S(2)}) %copy-start.1) | copy-done | bytes 8216
  18.0 1.5 %shard_map.60 = (f32[4,16,32]{2,1,0:T(8,128)}, f32[4,16,32]{2,1,0:T(8,128)}) custom-call(f32[16,128]{1,0:T(8,128)} %copy-done, f32[16,128]{1,0:T(8,128)} %copy-done.1), custom_call_target="tpu_custom_call" | custom-call | tf_op jit(solution)/shard_map/pallas_call | solution.py:338
Async XLA Ops:
  16.8 0.6 %copy-start = (f32[16,128]{1,0:T(8,128)}, f32[16,128]{1,0:T(8,128)S(1)}, u32[]{:S(2)}) copy-start(f32[16,128]{1,0:T(8,128)S(1)} %get-tuple-element.4.left_ref) | copy-start | bytes 24580
  17.4 0.6 %copy-start.1 = (f32[16,128]{1,0:T(8,128)}, f32[16,128]{1,0:T(8,128)S(1)}, u32[]{:S(2)}) copy-start(f32[16,128]{1,0:T(8,128)S(1)} %get-tuple-element.5.right_ref) | copy-start | bytes 24580

commit v3 on v2

--- a/solution.py
+++ b/solution.py
@@ -25,7 +25,7 @@
 
 def kernel(
     rows, cols,
-    a_hbm, b_hbm, d_hbm, w_hbm, left_ref, right_ref,
+    a_hbm, b_hbm, d_hbm, w_hbm, out_ref,
     a_own, b_own, a_pack, b_pack, a_all, b_all, d_buf, w_buf, a_high, a_low, b_high, b_low,
     g_high, g_low, h_high, h_low,
     left_sum, right_sum, left_send, right_send, left_recv, right_recv,
@@ -63,48 +63,50 @@
     def signal(row, col):
         pl.semaphore_signal(barrier, inc=1, device_id=(row, col), device_id_type=MESH)
 
-    def unless_self(row, col, act, mine=None):
-        same = jnp.logical_and(row == r, col == q)
-        pl.when(jnp.logical_not(same))(act)
-        if mine is not None:
-            pl.when(same)(mine)
-
-    for k in range(cols):
-        unless_self(owner_row, k, functools.partial(signal, owner_row, k))
-    for k in range(rows):
-        for h in range(halves):
-            col = r * halves + h
-            unless_self(k, col, functools.partial(signal, k, col))
+    def arrived(ref, sem):
+        pltpu.make_async_copy(ref, ref, sem).wait()
+
+    def owners(act, own):
+        for step in range(1, cols):
+            act((q + step) % cols, 0)
+        pl.when(jnp.logical_not(inside))(lambda: act(q, 1))
+        if own is not None:
+            pl.when(inside)(own)
+
+    def sources(act, own):
+        for step in range(1, rows):
+            for h in range(halves):
+                act((r + step) % rows, h, 0)
+        for step in range(1, halves):
+            act(r, (part + step) % halves, 0)
+        pl.when(jnp.logical_not(inside))(lambda: act(r, part, 1))
+        if own is not None:
+            pl.when(inside)(own)
+
+    owners(lambda col, _: signal(owner_row, col), None)
+    sources(lambda row, h, _: signal(row, r * halves + h), None)
     for step in range(1, rows):
         signal((r + step) % rows, q)
 
     fetch_b.wait()
     b_pack[...] = jnp.concatenate([b_own[s] for s in range(seqs)], axis=1)
-    b_all[r] = b_pack[...]
     fetch_a.wait()
     a_pack[...] = jnp.concatenate([a_own[s] for s in range(seqs)], axis=1)
 
-    @pl.when(inside)
-    def _():
-        a_all[part, r] = a_pack[...]
-
     pl.semaphore_wait(barrier, (rows - 1) + 2 * jnp.where(inside, cols - 1, cols))
 
-    def copy_b(step):
-        dest = (r + step) % rows
-        return pltpu.make_async_remote_copy(
-            src_ref=b_pack, dst_ref=b_all.at[r], send_sem=b_send_sem.at[step],
-            recv_sem=b_recv_sem.at[r], device_id=(dest, q), device_id_type=MESH)
-
-    def copy_a(k):
-        return pltpu.make_async_remote_copy(
-            src_ref=a_pack, dst_ref=a_all.at[part, r], send_sem=a_send_sem.at[k],
-            recv_sem=a_recv_sem.at[part, r], device_id=(owner_row, k), device_id_type=MESH)
-
     for step in range(1, rows):
-        copy_b(step).start()
-    for k in range(cols):
-        unless_self(owner_row, k, lambda k=k: copy_a(k).start())
+        pltpu.make_async_remote_copy(
+            src_ref=b_pack, dst_ref=b_all.at[r], send_sem=b_send_sem, recv_sem=b_recv_sem,
+            device_id=((r + step) % rows, q), device_id_type=MESH).start()
+    pltpu.make_async_copy(b_pack, b_all.at[r], b_recv_sem).start()
+
+    def send_a(col, which):
+        pltpu.make_async_remote_copy(
+            src_ref=a_pack, dst_ref=a_all.at[part, r], send_sem=a_send_sem.at[which],
+            recv_sem=a_recv_sem, device_id=(owner_row, col), device_id_type=MESH).start()
+
+    owners(send_a, lambda: pltpu.make_async_copy(a_pack, a_all.at[part, r], a_recv_sem).start())
 
     copy_d.wait()
     copy_w.wait()
@@ -168,11 +170,7 @@
         return [jnp.concatenate([y[:, h * width:(h + 1) * width] for y in x], axis=1)
                 for h in range(parts)]
 
-    for step in range(1, rows):
-        source = (r + step) % rows
-        pltpu.make_async_remote_copy(
-            src_ref=b_pack, dst_ref=b_all.at[source], send_sem=b_send_sem.at[step],
-            recv_sem=b_recv_sem.at[source], device_id=(source, q), device_id_type=MESH).wait_recv()
+    arrived(b_all, b_recv_sem)
     repeat_lanes(b_all[...].reshape(rows * res, LANES), feats_e, b_high, b_low, 0)
     mask_c = masks(group_c, feats_e)
 
@@ -189,27 +187,15 @@
         for h, piece in enumerate(pieces(left_sum, k, group_c, halves, chunks_c * res)):
             left_send[k, h] = piece
 
-    def copy_l(k, h):
-        return pltpu.make_async_remote_copy(
-            src_ref=left_send.at[k, h], dst_ref=left_recv.at[q], send_sem=l_send_sem.at[k, h],
-            recv_sem=l_recv_sem.at[q], device_id=(k, r * halves + h), device_id_type=MESH)
-
-    for k in range(rows):
-        for h in range(halves):
-            def mine(k=k, h=h):
-                left_recv[q] = left_send[k, h]
-
-            unless_self(k, r * halves + h, lambda k=k, h=h: copy_l(k, h).start(), mine)
-
-    for k in range(rows):
-        for h in range(halves):
-            def arrive(k=k, h=h):
-                pltpu.make_async_remote_copy(
-                    src_ref=a_pack, dst_ref=a_all.at[h, k], send_sem=a_send_sem.at[0],
-                    recv_sem=a_recv_sem.at[h, k], device_id=(k, r * halves + h),
-                    device_id_type=MESH).wait_recv()
-
-            unless_self(k, r * halves + h, arrive)
+    def send_l(row, h, which):
+        pltpu.make_async_remote_copy(
+            src_ref=left_send.at[row, h], dst_ref=left_recv.at[q], send_sem=l_send_sem.at[which],
+            recv_sem=l_recv_sem, device_id=(row, r * halves + h), device_id_type=MESH).start()
+
+    sources(send_l, lambda: pltpu.make_async_copy(
+        left_send.at[r, part], left_recv.at[q], l_recv_sem).start())
+
+    arrived(a_all, a_recv_sem)
     for h in range(halves):
         repeat_lanes(a_all[h].reshape(rows * res, LANES), feats, a_high, a_low, h * total * res)
     mask_e = masks(group_e, feats)
@@ -227,47 +213,35 @@
     right_sum[...] = jnp.concatenate([right] * (LANES // right.shape[1]), axis=1)
     for k in range(rows):
         right_send[k] = pieces(right_sum, k, group_e, 1, chunks_e * tile_j)[0]
-    right_recv[r] = right_send[r]
-
-    def copy_r(step):
+    for step in range(1, rows):
         dest = (r + step) % rows
-        return pltpu.make_async_remote_copy(
-            src_ref=right_send.at[dest], dst_ref=right_recv.at[r], send_sem=r_send_sem.at[step],
-            recv_sem=r_recv_sem.at[r], device_id=(dest, q), device_id_type=MESH)
-
-    for step in range(1, rows):
-        copy_r(step).start()
-
-    for k in range(cols):
-        def arrive(k=k):
-            pltpu.make_async_remote_copy(
-                src_ref=left_send.at[0, 0], dst_ref=left_recv.at[k], send_sem=l_send_sem.at[0, 0],
-                recv_sem=l_recv_sem.at[k], device_id=(owner_row, k),
-                device_id_type=MESH).wait_recv()
-
-        unless_self(owner_row, k, arrive)
-    left_ref[...] = jnp.sum(left_recv[...], axis=0) / total
-
-    for step in range(1, rows):
-        source = (r + step) % rows
         pltpu.make_async_remote_copy(
-            src_ref=right_send.at[source], dst_ref=right_recv.at[source],
-            send_sem=r_send_sem.at[step], recv_sem=r_recv_sem.at[source],
-            device_id=(source, q), device_id_type=MESH).wait_recv()
-    right_ref[...] = jnp.sum(right_recv[...], axis=0) / total
-
-    for step in range(1, rows):
-        copy_b(step).wait_send()
-        copy_r(step).wait_send()
-    for k in range(cols):
-        unless_self(owner_row, k, lambda k=k: copy_a(k).wait_send())
-    for k in range(rows):
-        for h in range(halves):
-            unless_self(k, r * halves + h, lambda k=k, h=h: copy_l(k, h).wait_send())
-
-
-def unfold(group_c, group_e, left_ref, right_ref, left_out, right_out):
-    for group, ref, out in ((group_c, left_ref, left_out), (group_e, right_ref, right_out)):
+            src_ref=right_send.at[dest], dst_ref=right_recv.at[r], send_sem=r_send_sem,
+            recv_sem=r_recv_sem, device_id=(dest, q), device_id_type=MESH).start()
+    pltpu.make_async_copy(right_send.at[r], right_recv.at[r], r_recv_sem).start()
+
+    arrived(left_recv, l_recv_sem)
+    size = left_recv.shape[1]
+    out_ref[:size, :] = jnp.sum(left_recv[...], axis=0) / total
+    arrived(right_recv, r_recv_sem)
+    out_ref[size:, :] = jnp.sum(right_recv[...], axis=0) / total
+
+    arrived(b_all.at[pl.ds(0, rows - 1)], b_send_sem)
+    arrived(right_recv.at[pl.ds(0, rows - 1)], r_send_sem)
+    arrived(left_recv.at[pl.ds(0, cols - 1)], l_send_sem.at[0])
+    arrived(d_buf.at[pl.ds(0, (cols - 1) * res)], a_send_sem.at[0])
+
+    @pl.when(jnp.logical_not(inside))
+    def _():
+        arrived(left_recv.at[0], l_send_sem.at[1])
+        arrived(a_pack, a_send_sem.at[1])
+
+
+def unfold(group_c, group_e, sums_ref, left_out, right_out):
+    size = left_out.size // LANES
+    for group, ref, out in (
+        (group_c, sums_ref.at[:size], left_out), (group_e, sums_ref.at[size:], right_out)
+    ):
         seqs, res, feats = out.shape
         x = ref[...].T
         each = ref.shape[0] // group
@@ -294,11 +268,11 @@
     left_piece = (seqs * feats * res // LANES, LANES)
     right_piece = (seqs * feats_e * res // LANES, LANES)
     dma = pltpu.SemaphoreType.DMA
-    left, right = pl.pallas_call(
+    sums = pl.pallas_call(
         functools.partial(kernel, rows, cols),
-        out_shape=(jax.ShapeDtypeStruct(left_piece, f32), jax.ShapeDtypeStruct(right_piece, f32)),
+        out_shape=jax.ShapeDtypeStruct((left_piece[0] + right_piece[0], LANES), f32),
         in_specs=[hbm] * 4,
-        out_specs=(vmem, vmem),
+        out_specs=vmem,
         scratch_shapes=[
             pltpu.VMEM(a.shape, f32),
             pltpu.VMEM(b.shape, f32),
@@ -323,24 +297,24 @@
             pltpu.VMEM((cols,) + left_piece, f32),
             pltpu.VMEM((rows,) + right_piece, f32),
             dma((4,)),
-            dma((cols,)),
-            dma((halves, rows)),
-            dma((rows,)),
-            dma((rows,)),
-            dma((rows, halves)),
-            dma((cols,)),
-            dma((rows,)),
-            dma((rows,)),
+            dma((2,)),
+            dma(()),
+            dma(()),
+            dma(()),
+            dma((2,)),
+            dma(()),
+            dma(()),
+            dma(()),
         ],
         compiler_params=pltpu.CompilerParams(
-            collective_id=0, has_side_effects=True, vmem_limit_bytes=54 * 2**20 - 101 * 2**10),
+            collective_id=0, has_side_effects=True, vmem_limit_bytes=54 * 2**20 - 117 * 2**10),
     )(a, b, d.reshape(pairs, pair), w)
     return pl.pallas_call(
         functools.partial(unfold, group_c, group_e),
         out_shape=(jax.ShapeDtypeStruct(a.shape, f32), jax.ShapeDtypeStruct(b.shape, f32)),
-        in_specs=[vmem] * 2,
+        in_specs=[vmem],
         out_specs=(vmem, vmem),
-    )(left, right)
+    )(sums)
 
 
 def solution(mesh):

time: 19.8 us -> 19.6 us (0.990)
  Pallas kernels: 17.7 us -> 17.3 us
    pallas_call x1, Pallas kernels: 16.2 us -> 15.8 us  [on_device(): pl.pallas_call(functools.partial(kernel, rows, cols), out_shape=jax.Shape...]
where the time goes in v3:
time: 19.6 us; the launch traced here: 19.3 us
  Pallas kernels  17.3 us (88%)
  local copies, waits for them, and re-layouts  1.34 us (7%)
  between operations  0.66 us (3%)
    pallas_call x1, Pallas kernels, on_device(): pl.pallas_call(functools.partial(kernel, rows, cols), out_shape=jax.Shape...  15.8 us
    pallas_call x1, Pallas kernels, on_device(): pl.pallas_call(functools.partial(unfold, group_c, group_e), out_shape=(ja...  1.54 us
    unnamed x4, local copies, waits for them, and re-layouts  1.34 us

profile of v3, /device:TPU:0, one launch (start us, length us, event | category | flops | bytes accessed | tf_op | source)
XLA Modules:
  0.0 19.3 jit_solution(17355839488156733772)
XLA Ops:
  0.6 0.0 copy-start.1
  0.6 0.7 %copy-done.1 = f32[4,16,32]{2,1,0:T(8,128)S(1)} copy-done((f32[4,16,32]{2,1,0:T(8,128)S(1)}, f32[4,16,32]{2,1,0:T(8,128)}, u32[]{:S(2)}) %copy-start.1) | copy-done | bytes 8216
  1.4 15.8 %shard_map.59.sums_ref = f32[32,128]{1,0:T(8,128)S(1)} custom-call(f32[4,16,32]{2,1,0:T(8,128)S(1)} %copy-done.1, f32[4,16,32]{2,1,0:T(8,128)} %b_hbm.1, f32[512,128]{1,0:T(8,128)} %bitcast.1, f32[1024,128]{1,0:T(8,128)} %w_hbm.1), custom_call_target="tpu_custom_call" | custom-call | tf_op jit(solution)/shard_map/pallas_call | solution.py:271
  17.2 0.0 copy-start
  17.2 0.6 %copy-done = f32[32,128]{1,0:T(8,128)} copy-done((f32[32,128]{1,0:T(8,128)}, f32[32,128]{1,0:T(8,128)S(1)}, u32[]{:S(2)}) %copy-start) | copy-done | bytes 16408
  17.8 1.5 %shard_map.60 = (f32[4,16,32]{2,1,0:T(8,128)}, f32[4,16,32]{2,1,0:T(8,128)}) custom-call(f32[32,128]{1,0:T(8,128)} %copy-done), custom_call_target="tpu_custom_call" | custom-call | tf_op jit(solution)/shard_map/pallas_call | solution.py:312
Async XLA Ops:
  0.6 0.8 %copy-start.1 = (f32[4,16,32]{2,1,0:T(8,128)S(1)}, f32[4,16,32]{2,1,0:T(8,128)}, u32[]{:S(2)}) copy-start(f32[4,16,32]{2,1,0:T(8,128)} %a_hbm.1) | copy-start | bytes 24580
  17.2 0.6 %copy-start = (f32[32,128]{1,0:T(8,128)}, f32[32,128]{1,0:T(8,128)S(1)}, u32[]{:S(2)}) copy-start(f32[32,128]{1,0:T(8,128)S(1)} %shard_map.59.sums_ref) | copy-start | bytes 49156

commit v4 on v3

--- a/solution.py
+++ b/solution.py
@@ -8,9 +8,10 @@
 from jax.sharding import PartitionSpec as P
 
 MESH = pl.DeviceIdType.MESH
-WIDE = 256
+WIDE = 128
+SPAN = 2
 LANES = 128
-DEPTH = 4
+DEPTH = 8
 
 
 def split(x):
@@ -27,7 +28,7 @@
     rows, cols,
     a_hbm, b_hbm, d_hbm, w_hbm, out_ref,
     a_own, b_own, a_pack, b_pack, a_all, b_all, d_buf, w_buf, a_high, a_low, b_high, b_low,
-    g_high, g_low, h_high, h_low,
+    g_buf, h_buf,
     left_sum, right_sum, left_send, right_send, left_recv, right_recv,
     local_sem, a_send_sem, a_recv_sem, b_send_sem, b_recv_sem,
     l_send_sem, l_recv_sem, r_send_sem, r_recv_sem,
@@ -114,22 +115,33 @@
     d_turned = jnp.concatenate(
         [d_buf[pl.ds(j, tile_i, stride=tile_j), :] for j in range(tile_j)], axis=0)
 
-    def expand(d, w, high_ref, low_ref, chunks):
+    def expand(d, w, chunks, place):
         d_high, d_low = split(d)
-        d_both = jnp.concatenate([d_high, d_low], axis=1)
-        for n in range(chunks):
-            w_high, w_low = split(w[n])
-            out = dot_nt(d_both, jnp.concatenate([w_high, w_high], axis=1))
-            out = out + dot_nt(d_high, w_low)
-            out_high, out_low = split(out)
-            high_ref[n] = out_high
-            low_ref[n] = out_low
-
-    expand(d_turned, [w_buf[n * WIDE:(n + 1) * WIDE, :] for n in range(chunks_c)],
-           g_high, g_low, chunks_c)
-    expand(d_plain, [jnp.concatenate(
-        [w_buf[pl.ds(n * group_e + e, feats, stride=feats_e), :] for e in range(group_e)], axis=0)
-        for n in range(chunks_e)], h_high, h_low, chunks_e)
+        d_all = jnp.concatenate([d_high, d_low, d_high], axis=1)
+        for first in range(0, chunks, SPAN):
+            group = range(first, min(first + SPAN, chunks))
+            w_high, w_low = split(jnp.concatenate([w(n) for n in group], axis=0))
+            out = dot_nt(d_all, jnp.concatenate([w_high, w_high, w_low], axis=1))
+            for low, value in enumerate(split(out)):
+                for n in group:
+                    place(low, n, value[:, (n - first) * WIDE:(n - first + 1) * WIDE])
+
+    def place_g(low, n, value):
+        for j in range(tile_j):
+            for h in range(halves):
+                top = ((low * halves + h) * chunks_c + n) * res
+                g_buf[top:top + res, j * WIDE:(j + 1) * WIDE] = value[
+                    j * tile_i + h * res:j * tile_i + (h + 1) * res]
+
+    def place_h(low, n, value):
+        top = (low * chunks_e + n) * tile_j
+        for i in range(tile_i):
+            h_buf[top:top + tile_j, i * WIDE:(i + 1) * WIDE] = value[i * tile_j:(i + 1) * tile_j]
+
+    expand(d_turned, lambda n: w_buf[n * WIDE:(n + 1) * WIDE, :], chunks_c, place_g)
+    expand(d_plain, lambda n: jnp.concatenate(
+        [w_buf[pl.ds(n * group_e + e, feats, stride=feats_e), :] for e in range(group_e)], axis=0),
+        chunks_e, place_h)
 
     def repeat_lanes(x, width, high_ref, low_ref, base):
         size = x.shape[0]
@@ -148,27 +160,21 @@
 
     def spread(ref, start, mask):
         x = ref[pl.ds(start, total, stride=res), :].astype(jnp.bfloat16)
-        x = jnp.concatenate([x] * (WIDE // LANES), axis=1)
         return jnp.concatenate([x * mask[k:k + 1] for k in range(mask.shape[0])], axis=0)
 
     def contract(count, coef, mat):
         acc = None
         for first in range(0, count, DEPTH):
-            steps = range(first, min(first + DEPTH, count))
-            lhs = jnp.concatenate([coef(n) for n in steps], axis=1)
-            rhs = jnp.concatenate([mat(n) for n in steps], axis=1)
-            term = dot_nt(lhs, rhs)
+            last = min(first + DEPTH, count)
+            lhs = jnp.concatenate([coef(n) for n in range(first, last)], axis=1)
+            term = dot_nt(lhs, mat[:, first * WIDE:last * WIDE])
             acc = term if acc is None else acc + term
         size, width = acc.shape[0] // 2, acc.shape[1] // 2
         return acc[:size, :width] + acc[:size, width:] + acc[size:, :width]
 
-    def pieces(ref, k, group, parts, width):
-        fold = LANES // width
-        x = [ref[pl.ds(s * rows + k, group, stride=total), :] for s in range(seqs)]
-        each = seqs // fold
-        x = [jnp.concatenate(x[u * each:(u + 1) * each], axis=0) for u in range(fold)]
-        return [jnp.concatenate([y[:, h * width:(h + 1) * width] for y in x], axis=1)
-                for h in range(parts)]
+    def piece(ref, k, group):
+        return jnp.concatenate(
+            [ref[pl.ds(s * rows + k, group, stride=total), :] for s in range(seqs)], axis=0)
 
     arrived(b_all, b_recv_sem)
     repeat_lanes(b_all[...].reshape(rows * res, LANES), feats_e, b_high, b_low, 0)
@@ -177,15 +183,12 @@
     def left_coef(j):
         return jnp.concatenate([spread(b_high, j, mask_c), spread(b_low, j, mask_c)], axis=0)
 
-    def left_mat(j):
-        return jnp.concatenate(
-            [ref[n, j * tile_i + h * res:j * tile_i + (h + 1) * res, :]
-             for ref in (g_high, g_low) for h in range(halves) for n in range(chunks_c)], axis=0)
-
-    left_sum[...] = contract(tile_j, left_coef, left_mat)
+    left = contract(tile_j, left_coef, g_buf)
+    for h in range(halves):
+        left_sum[h] = left[:, h * LANES:(h + 1) * LANES]
     for k in range(rows):
-        for h, piece in enumerate(pieces(left_sum, k, group_c, halves, chunks_c * res)):
-            left_send[k, h] = piece
+        for h in range(halves):
+            left_send[k, h] = piece(left_sum.at[h], k, group_c)
 
     def send_l(row, h, which):
         pltpu.make_async_remote_copy(
@@ -204,15 +207,10 @@
         start = (i // res) * total * res + i % res
         return jnp.concatenate([spread(a_high, start, mask_e), spread(a_low, start, mask_e)], axis=0)
 
-    def right_mat(i):
-        span = slice(i * tile_j, (i + 1) * tile_j)
-        return jnp.concatenate(
-            [ref[n, span, :] for ref in (h_high, h_low) for n in range(chunks_e)], axis=0)
-
-    right = contract(tile_i, right_coef, right_mat)
-    right_sum[...] = jnp.concatenate([right] * (LANES // right.shape[1]), axis=1)
+    right_sum[...] = contract(tile_i, right_coef, h_buf)
     for k in range(rows):
-        right_send[k] = pieces(right_sum, k, group_e, 1, chunks_e * tile_j)[0]
+        right_send[k] = piece(right_sum, k, group_e)
+
     for step in range(1, rows):
         dest = (r + step) % rows
         pltpu.make_async_remote_copy(
@@ -286,11 +284,9 @@
             pltpu.VMEM((total * tile_i, LANES), f32),
             pltpu.VMEM((total * tile_j, LANES), f32),
             pltpu.VMEM((total * tile_j, LANES), f32),
-            pltpu.VMEM((chunks_c, pairs, WIDE), bf16),
-            pltpu.VMEM((chunks_c, pairs, WIDE), bf16),
-            pltpu.VMEM((chunks_e, pairs, WIDE), bf16),
-            pltpu.VMEM((chunks_e, pairs, WIDE), bf16),
-            pltpu.VMEM((total * group_c, LANES), f32),
+            pltpu.VMEM((2 * chunks_c * tile_i, tile_j * WIDE), bf16),
+            pltpu.VMEM((2 * chunks_e * tile_j, tile_i * WIDE), bf16),
+            pltpu.VMEM((halves, total * group_c, LANES), f32),
             pltpu.VMEM((total * group_e, LANES), f32),
             pltpu.VMEM((rows, halves) + left_piece, f32),
             pltpu.VMEM((rows,) + right_piece, f32),
@@ -307,7 +303,7 @@
             dma(()),
         ],
         compiler_params=pltpu.CompilerParams(
-            collective_id=0, has_side_effects=True, vmem_limit_bytes=54 * 2**20 - 117 * 2**10),
+            collective_id=0, has_side_effects=True, vmem_limit_bytes=60 * 2**20),
     )(a, b, d.reshape(pairs, pair), w)
     return pl.pallas_call(
         functools.partial(unfold, group_c, group_e),

time: 19.6 us -> 18.3 us (0.934)
  local copies, waits for them, and re-layouts: 1.34 us -> 0 us
    unnamed x4 -> x0, local copies, waits for them, and re-layouts: 1.34 us -> none
where the time goes in v4:
time: 18.3 us; the launch traced here: 18.1 us
  Pallas kernels  17.4 us (95%)
  between operations  0.64 us (3%)
    pallas_call x1, Pallas kernels, on_device(): pl.pallas_call(functools.partial(kernel, rows, cols), out_shape=jax.Shape...  15.8 us
    pallas_call x1, Pallas kernels, on_device(): pl.pallas_call(functools.partial(unfold, group_c, group_e), out_shape=(ja...  1.65 us

profile of v4, /device:TPU:0, one launch (start us, length us, event | category | flops | bytes accessed | tf_op | source)
XLA Modules:
  0.0 18.1 jit_solution(10599471791030785386)
XLA Ops:
  0.6 15.8 %shard_map.59.sums_ref = f32[32,128]{1,0:T(8,128)} custom-call(f32[4,16,32]{2,1,0:T(8,128)} %a_hbm.1, f32[4,16,32]{2,1,0:T(8,128)} %b_hbm.1, f32[512,128]{1,0:T(8,128)} %bitcast.1, f32[1024,128]{1,0:T(8,128)} %w_hbm.1), custom_call_target="tpu_custom_call" | custom-call | tf_op jit(solution)/shard_map/pallas_call | solution.py:269
  16.4 1.6 %shard_map.60 = (f32[4,16,32]{2,1,0:T(8,128)}, f32[4,16,32]{2,1,0:T(8,128)}) custom-call(f32[32,128]{1,0:T(8,128)} %shard_map.59.sums_ref), custom_call_target="tpu_custom_call" | custom-call | tf_op jit(solution)/shard_map/pallas_call | solution.py:308

commit v5 on v4

--- a/solution.py
+++ b/solution.py
@@ -84,7 +84,6 @@
         if own is not None:
             pl.when(inside)(own)
 
-    owners(lambda col, _: signal(owner_row, col), None)
     sources(lambda row, h, _: signal(row, r * halves + h), None)
     for step in range(1, rows):
         signal((r + step) % rows, q)
@@ -94,20 +93,20 @@
     fetch_a.wait()
     a_pack[...] = jnp.concatenate([a_own[s] for s in range(seqs)], axis=1)
 
-    pl.semaphore_wait(barrier, (rows - 1) + 2 * jnp.where(inside, cols - 1, cols))
+    pl.semaphore_wait(barrier, (rows - 1) + jnp.where(inside, cols - 1, cols))
+
+    def send_a(col, which):
+        pltpu.make_async_remote_copy(
+            src_ref=a_pack, dst_ref=a_all.at[part, r], send_sem=a_send_sem.at[which],
+            recv_sem=a_recv_sem, device_id=(owner_row, col), device_id_type=MESH).start()
+
+    owners(send_a, lambda: pltpu.make_async_copy(a_pack, a_all.at[part, r], a_recv_sem).start())
 
     for step in range(1, rows):
         pltpu.make_async_remote_copy(
             src_ref=b_pack, dst_ref=b_all.at[r], send_sem=b_send_sem, recv_sem=b_recv_sem,
             device_id=((r + step) % rows, q), device_id_type=MESH).start()
     pltpu.make_async_copy(b_pack, b_all.at[r], b_recv_sem).start()
-
-    def send_a(col, which):
-        pltpu.make_async_remote_copy(
-            src_ref=a_pack, dst_ref=a_all.at[part, r], send_sem=a_send_sem.at[which],
-            recv_sem=a_recv_sem, device_id=(owner_row, col), device_id_type=MESH).start()
-
-    owners(send_a, lambda: pltpu.make_async_copy(a_pack, a_all.at[part, r], a_recv_sem).start())
 
     copy_d.wait()
     copy_w.wait()
@@ -195,10 +194,10 @@
             src_ref=left_send.at[row, h], dst_ref=left_recv.at[q], send_sem=l_send_sem.at[which],
             recv_sem=l_recv_sem, device_id=(row, r * halves + h), device_id_type=MESH).start()
 
+    arrived(a_all, a_recv_sem)
     sources(send_l, lambda: pltpu.make_async_copy(
         left_send.at[r, part], left_recv.at[q], l_recv_sem).start())
 
-    arrived(a_all, a_recv_sem)
     for h in range(halves):
         repeat_lanes(a_all[h].reshape(rows * res, LANES), feats, a_high, a_low, h * total * res)
     mask_e = masks(group_e, feats)

time: 18.3 us -> 19.2 us (1.049)
  Pallas kernels: 17.4 us -> 18.3 us
    pallas_call x1, Pallas kernels: 15.8 us -> 16.6 us  [on_device(): pl.pallas_call(functools.partial(kernel, rows, cols), out_shape=jax.Shape...]
where the time goes in v5:
time: 19.2 us; the launch traced here: 18.9 us
  Pallas kernels  18.3 us (95%)
  between operations  0.64 us (3%)
    pallas_call x1, Pallas kernels, on_device(): pl.pallas_call(functools.partial(kernel, rows, cols), out_shape=jax.Shape...  16.6 us
    pallas_call x1, Pallas kernels, on_device(): pl.pallas_call(functools.partial(unfold, group_c, group_e), out_shape=(ja...  1.65 us

profile of v5, /device:TPU:0, one launch (start us, length us, event | category | flops | bytes accessed | tf_op | source)
XLA Modules:
  0.0 18.9 jit_solution(15727750005984696109)
XLA Ops:
  0.6 16.6 %shard_map.59.sums_ref = f32[32,128]{1,0:T(8,128)} custom-call(f32[4,16,32]{2,1,0:T(8,128)} %a_hbm.1, f32[4,16,32]{2,1,0:T(8,128)} %b_hbm.1, f32[512,128]{1,0:T(8,128)} %bitcast.1, f32[1024,128]{1,0:T(8,128)} %w_hbm.1), custom_call_target="tpu_custom_call" | custom-call | tf_op jit(solution)/shard_map/pallas_call | solution.py:268
  17.3 1.6 %shard_map.60 = (f32[4,16,32]{2,1,0:T(8,128)}, f32[4,16,32]{2,1,0:T(8,128)}) custom-call(f32[32,128]{1,0:T(8,128)} %shard_map.59.sums_ref), custom_call_target="tpu_custom_call" | custom-call | tf_op jit(solution)/shard_map/pallas_call | solution.py:307

commit v6 on v5

--- a/solution.py
+++ b/solution.py
@@ -28,7 +28,7 @@
     rows, cols,
     a_hbm, b_hbm, d_hbm, w_hbm, out_ref,
     a_own, b_own, a_pack, b_pack, a_all, b_all, d_buf, w_buf, a_high, a_low, b_high, b_low,
-    g_buf, h_buf,
+    g_buf, h_buf, unit_a, unit_b,
     left_sum, right_sum, left_send, right_send, left_recv, right_recv,
     local_sem, a_send_sem, a_recv_sem, b_send_sem, b_recv_sem,
     l_send_sem, l_recv_sem, r_send_sem, r_recv_sem,
@@ -108,6 +108,21 @@
             device_id=((r + step) % rows, q), device_id_type=MESH).start()
     pltpu.make_async_copy(b_pack, b_all.at[r], b_recv_sem).start()
 
+    for unit, width in ((unit_a, feats), (unit_b, feats_e)):
+        lane = lax.broadcasted_iota(jnp.int32, (LANES, LANES), 1)
+        offset = lax.broadcasted_iota(jnp.int32, (LANES, LANES), 0) - lax.rem(lane, width)
+        for s in range(seqs):
+            unit[:, s * LANES:(s + 1) * LANES] = (offset == s * width).astype(
+                jnp.float32).astype(jnp.bfloat16)
+
+    def masks(group, width):
+        lane = lax.broadcasted_iota(jnp.int32, (group, WIDE), 1) // width
+        block = lax.broadcasted_iota(jnp.int32, (group, WIDE), 0)
+        return (lane == block).astype(jnp.float32).astype(jnp.bfloat16)
+
+    mask_c = masks(group_c, feats_e)
+    mask_e = masks(group_e, feats)
+
     copy_d.wait()
     copy_w.wait()
     d_plain = d_buf[...]
@@ -142,20 +157,14 @@
         [w_buf[pl.ds(n * group_e + e, feats, stride=feats_e), :] for e in range(group_e)], axis=0),
         chunks_e, place_h)
 
-    def repeat_lanes(x, width, high_ref, low_ref, base):
-        size = x.shape[0]
-        source = lax.broadcasted_iota(jnp.int32, (LANES, seqs * LANES), 0)
-        target = lax.broadcasted_iota(jnp.int32, (LANES, seqs * LANES), 1)
-        unit = (source == target // LANES * width + target % width).astype(jnp.bfloat16)
+    def repeat_lanes(x, unit, parts, high_ref, low_ref):
+        size = x.shape[0] // parts
         for part_of, ref in zip(split(x), (high_ref, low_ref)):
-            out = jnp.dot(part_of, unit, preferred_element_type=jnp.float32)
-            for s in range(seqs):
-                ref[base + s * size:base + (s + 1) * size, :] = out[:, s * LANES:(s + 1) * LANES]
-
-    def masks(group, width):
-        lane = lax.broadcasted_iota(jnp.int32, (group, WIDE), 1) // width
-        block = lax.broadcasted_iota(jnp.int32, (group, WIDE), 0)
-        return (lane == block).astype(jnp.float32).astype(jnp.bfloat16)
+            out = jnp.dot(part_of, unit[...], preferred_element_type=jnp.float32)
+            for h in range(parts):
+                for s in range(seqs):
+                    ref[(h * seqs + s) * size:(h * seqs + s + 1) * size, :] = out[
+                        h * size:(h + 1) * size, s * LANES:(s + 1) * LANES]
 
     def spread(ref, start, mask):
         x = ref[pl.ds(start, total, stride=res), :].astype(jnp.bfloat16)
@@ -176,8 +185,7 @@
             [ref[pl.ds(s * rows + k, group, stride=total), :] for s in range(seqs)], axis=0)
 
     arrived(b_all, b_recv_sem)
-    repeat_lanes(b_all[...].reshape(rows * res, LANES), feats_e, b_high, b_low, 0)
-    mask_c = masks(group_c, feats_e)
+    repeat_lanes(b_all[...].reshape(rows * res, LANES), unit_b, 1, b_high, b_low)
 
     def left_coef(j):
         return jnp.concatenate([spread(b_high, j, mask_c), spread(b_low, j, mask_c)], axis=0)
@@ -198,9 +206,7 @@
     sources(send_l, lambda: pltpu.make_async_copy(
         left_send.at[r, part], left_recv.at[q], l_recv_sem).start())
 
-    for h in range(halves):
-        repeat_lanes(a_all[h].reshape(rows * res, LANES), feats, a_high, a_low, h * total * res)
-    mask_e = masks(group_e, feats)
+    repeat_lanes(a_all[...].reshape(halves * rows * res, LANES), unit_a, halves, a_high, a_low)
 
     def right_coef(i):
         start = (i // res) * total * res + i % res
@@ -285,6 +291,8 @@
             pltpu.VMEM((total * tile_j, LANES), f32),
             pltpu.VMEM((2 * chunks_c * tile_i, tile_j * WIDE), bf16),
             pltpu.VMEM((2 * chunks_e * tile_j, tile_i * WIDE), bf16),
+            pltpu.VMEM((LANES, seqs * LANES), bf16),
+            pltpu.VMEM((LANES, seqs * LANES), bf16),
             pltpu.VMEM((halves, total * group_c, LANES), f32),
             pltpu.VMEM((total * group_e, LANES), f32),
             pltpu.VMEM((rows, halves) + left_piece, f32),

time: 19.2 us -> 19.2 us (level)
  no operation moved by 1% of the time
where the time goes in v6:
time: 19.2 us; the launch traced here: 18.9 us
  Pallas kernels  18.3 us (95%)
  between operations  0.64 us (3%)
    pallas_call x1, Pallas kernels, on_device(): pl.pallas_call(functools.partial(kernel, rows, cols), out_shape=jax.Shape...  16.6 us
    pallas_call x1, Pallas kernels, on_device(): pl.pallas_call(functools.partial(unfold, group_c, group_e), out_shape=(ja...  1.65 us

profile of v6, /device:TPU:0, one launch (start us, length us, event | category | flops | bytes accessed | tf_op | source)
XLA Modules:
  0.0 18.9 jit_solution(10116922753306095062)
XLA Ops:
  0.6 16.6 %shard_map.59.sums_ref = f32[32,128]{1,0:T(8,128)} custom-call(f32[4,16,32]{2,1,0:T(8,128)} %a_hbm.1, f32[4,16,32]{2,1,0:T(8,128)} %b_hbm.1, f32[512,128]{1,0:T(8,128)} %bitcast.1, f32[1024,128]{1,0:T(8,128)} %w_hbm.1), custom_call_target="tpu_custom_call" | custom-call | tf_op jit(solution)/shard_map/pallas_call | solution.py:274
  17.3 1.6 %shard_map.60 = (f32[4,16,32]{2,1,0:T(8,128)}, f32[4,16,32]{2,1,0:T(8,128)}) custom-call(f32[32,128]{1,0:T(8,128)} %shard_map.59.sums_ref), custom_call_target="tpu_custom_call" | custom-call | tf_op jit(solution)/shard_map/pallas_call | solution.py:315

commit v7 on v4

--- a/solution.py
+++ b/solution.py
@@ -89,26 +89,6 @@
     for step in range(1, rows):
         signal((r + step) % rows, q)
 
-    fetch_b.wait()
-    b_pack[...] = jnp.concatenate([b_own[s] for s in range(seqs)], axis=1)
-    fetch_a.wait()
-    a_pack[...] = jnp.concatenate([a_own[s] for s in range(seqs)], axis=1)
-
-    pl.semaphore_wait(barrier, (rows - 1) + 2 * jnp.where(inside, cols - 1, cols))
-
-    for step in range(1, rows):
-        pltpu.make_async_remote_copy(
-            src_ref=b_pack, dst_ref=b_all.at[r], send_sem=b_send_sem, recv_sem=b_recv_sem,
-            device_id=((r + step) % rows, q), device_id_type=MESH).start()
-    pltpu.make_async_copy(b_pack, b_all.at[r], b_recv_sem).start()
-
-    def send_a(col, which):
-        pltpu.make_async_remote_copy(
-            src_ref=a_pack, dst_ref=a_all.at[part, r], send_sem=a_send_sem.at[which],
-            recv_sem=a_recv_sem, device_id=(owner_row, col), device_id_type=MESH).start()
-
-    owners(send_a, lambda: pltpu.make_async_copy(a_pack, a_all.at[part, r], a_recv_sem).start())
-
     copy_d.wait()
     copy_w.wait()
     d_plain = d_buf[...]
@@ -139,6 +119,26 @@
             h_buf[top:top + tile_j, i * WIDE:(i + 1) * WIDE] = value[i * tile_j:(i + 1) * tile_j]
 
     expand(d_turned, lambda n: w_buf[n * WIDE:(n + 1) * WIDE, :], chunks_c, place_g)
+    fetch_b.wait()
+    b_pack[...] = jnp.concatenate([b_own[s] for s in range(seqs)], axis=1)
+    fetch_a.wait()
+    a_pack[...] = jnp.concatenate([a_own[s] for s in range(seqs)], axis=1)
+
+    pl.semaphore_wait(barrier, (rows - 1) + 2 * jnp.where(inside, cols - 1, cols))
+
+    for step in range(1, rows):
+        pltpu.make_async_remote_copy(
+            src_ref=b_pack, dst_ref=b_all.at[r], send_sem=b_send_sem, recv_sem=b_recv_sem,
+            device_id=((r + step) % rows, q), device_id_type=MESH).start()
+    pltpu.make_async_copy(b_pack, b_all.at[r], b_recv_sem).start()
+
+    def send_a(col, which):
+        pltpu.make_async_remote_copy(
+            src_ref=a_pack, dst_ref=a_all.at[part, r], send_sem=a_send_sem.at[which],
+            recv_sem=a_recv_sem, device_id=(owner_row, col), device_id_type=MESH).start()
+
+    owners(send_a, lambda: pltpu.make_async_copy(a_pack, a_all.at[part, r], a_recv_sem).start())
+
     expand(d_plain, lambda n: jnp.concatenate(
         [w_buf[pl.ds(n * group_e + e, feats, stride=feats_e), :] for e in range(group_e)], axis=0),
         chunks_e, place_h)

time: 18.3 us -> 18.9 us (1.033)
  Pallas kernels: 17.4 us -> 18 us
    pallas_call x1, Pallas kernels: 15.8 us -> 16.4 us  [on_device(): pl.pallas_call(functools.partial(kernel, rows, cols), out_shape=jax.Shape...]
where the time goes in v7:
time: 18.9 us; the launch traced here: 18.7 us
  Pallas kernels  18 us (95%)
  between operations  0.64 us (3%)
    pallas_call x1, Pallas kernels, on_device(): pl.pallas_call(functools.partial(kernel, rows, cols), out_shape=jax.Shape...  16.4 us
    pallas_call x1, Pallas kernels, on_device(): pl.pallas_call(functools.partial(unfold, group_c, group_e), out_shape=(ja...  1.65 us

profile of v7, /device:TPU:0, one launch (start us, length us, event | category | flops | bytes accessed | tf_op | source)
XLA Modules:
  0.0 18.7 jit_solution(8153340587619179808)
XLA Ops:
  0.6 16.4 %shard_map.59.sums_ref = f32[32,128]{1,0:T(8,128)} custom-call(f32[4,16,32]{2,1,0:T(8,128)} %a_hbm.1, f32[4,16,32]{2,1,0:T(8,128)} %b_hbm.1, f32[512,128]{1,0:T(8,128)} %bitcast.1, f32[1024,128]{1,0:T(8,128)} %w_hbm.1), custom_call_target="tpu_custom_call" | custom-call | tf_op jit(solution)/shard_map/pallas_call | solution.py:269
  17.0 1.6 %shard_map.60 = (f32[4,16,32]{2,1,0:T(8,128)}, f32[4,16,32]{2,1,0:T(8,128)}) custom-call(f32[32,128]{1,0:T(8,128)} %shard_map.59.sums_ref), custom_call_target="tpu_custom_call" | custom-call | tf_op jit(solution)/shard_map/pallas_call | solution.py:308

commit v8 on v4

--- a/solution.py
+++ b/solution.py
@@ -139,9 +139,6 @@
             h_buf[top:top + tile_j, i * WIDE:(i + 1) * WIDE] = value[i * tile_j:(i + 1) * tile_j]
 
     expand(d_turned, lambda n: w_buf[n * WIDE:(n + 1) * WIDE, :], chunks_c, place_g)
-    expand(d_plain, lambda n: jnp.concatenate(
-        [w_buf[pl.ds(n * group_e + e, feats, stride=feats_e), :] for e in range(group_e)], axis=0),
-        chunks_e, place_h)
 
     def repeat_lanes(x, width, high_ref, low_ref, base):
         size = x.shape[0]
@@ -198,6 +195,9 @@
     sources(send_l, lambda: pltpu.make_async_copy(
         left_send.at[r, part], left_recv.at[q], l_recv_sem).start())
 
+    expand(d_plain, lambda n: jnp.concatenate(
+        [w_buf[pl.ds(n * group_e + e, feats, stride=feats_e), :] for e in range(group_e)], axis=0),
+        chunks_e, place_h)
     arrived(a_all, a_recv_sem)
     for h in range(halves):
         repeat_lanes(a_all[h].reshape(rows * res, LANES), feats, a_high, a_low, h * total * res)

time: 18.3 us -> 18.9 us (1.033)
  Pallas kernels: 17.4 us -> 18 us
    pallas_call x1, Pallas kernels: 15.8 us -> 16.4 us  [on_device(): pl.pallas_call(functools.partial(kernel, rows, cols), out_shape=jax.Shape...]
where the time goes in v8:
time: 18.9 us; the launch traced here: 18.6 us
  Pallas kernels  18 us (95%)
  between operations  0.64 us (3%)
    pallas_call x1, Pallas kernels, on_device(): pl.pallas_call(functools.partial(kernel, rows, cols), out_shape=jax.Shape...  16.4 us
    pallas_call x1, Pallas kernels, on_device(): pl.pallas_call(functools.partial(unfold, group_c, group_e), out_shape=(ja...  1.65 us

profile of v8, /device:TPU:0, one launch (start us, length us, event | category | flops | bytes accessed | tf_op | source)
XLA Modules:
  0.0 18.6 jit_solution(8228316472613463410)
XLA Ops:
  0.6 16.4 %shard_map.59.sums_ref = f32[32,128]{1,0:T(8,128)} custom-call(f32[4,16,32]{2,1,0:T(8,128)} %a_hbm.1, f32[4,16,32]{2,1,0:T(8,128)} %b_hbm.1, f32[512,128]{1,0:T(8,128)} %bitcast.1, f32[1024,128]{1,0:T(8,128)} %w_hbm.1), custom_call_target="tpu_custom_call" | custom-call | tf_op jit(solution)/shard_map/pallas_call | solution.py:269
  17.0 1.6 %shard_map.60 = (f32[4,16,32]{2,1,0:T(8,128)}, f32[4,16,32]{2,1,0:T(8,128)}) custom-call(f32[32,128]{1,0:T(8,128)} %shard_map.59.sums_ref), custom_call_target="tpu_custom_call" | custom-call | tf_op jit(solution)/shard_map/pallas_call | solution.py:308
